TPU v7x, 32 devices: a whole 2x2x4 slice. The times are simulated.
32 devices in a mesh: grp: 4 (over x, core), tp: 8 (over z, y).
Axes of the slice: x: 2, y: 2, z: 4, core: 2. Of those that a mesh axis runs over, the one named last changes fastest.
Arguments:
- in_panels: bfloat16 [8, 1024, 2, 8192], P('grp', None, None, 'tp'), may hold values from -0.0625 to 0.0625
- layout: int32 [8], replicated, may hold values from 0 to 7, each once
- hidden: bfloat16 [128, 16, 8192], P('grp', None, 'tp'), may hold values from -6 to 6
- prompt_state: float32 [16, 19, 8192], P('grp', None, 'tp'), may hold values from -6 to 6
- fork_counts: int32 [4, 16], replicated, may hold values from 0 to 16, as said below
- conv_weight: float32 [4, 8192], P(None, 'tp'), may hold values from -0.8 to 0.8
- conv_bias: float32 [8192], P('tp'), may hold values from -0.5 to 0.5
- x_weight: bfloat16 [8192, 544], P('tp'), may hold values from -0.0625 to 0.0625
- dt_weight: bfloat16 [512, 8192], P(None, 'tp'), may hold values from -0.25 to 0.25
- dt_bias: float32 [8192], P('tp'), may hold values from -6 to -2
- decay_rate: float32 [16, 8192], P(None, 'tp'), may hold values from 0.5 to 8
- skip_gain: float32 [8192], P('tp'), may hold values from 0.5 to 1.5
Outputs:
- mixed: bfloat16 [128, 16, 8192], P('grp', None, 'tp')
- final_state: float32 [128, 19, 8192], P('grp', None, 'tp')
Inputs may be any that keep to these rules, and one draw needn't show every extreme that they name: `layout`: A permutation of the panel slots. Each row sums to 32: group g's sequences fork the prompts in order, prompt p taking fork_counts[g, p] of them. In every row some prompt takes exactly 16.
All inputs are finite; a program needn't handle non-finite values.
Results may differ from a plain program's by a relative error of at most 0.0069.
Values may be sent and summed in bfloat16 or wider, within the bound.
A program may use at most 192 MiB of HBM per device.

v0:
```python
import jax
import jax.numpy as jnp
from jax import lax
from jax.sharding import PartitionSpec as P


def fork_sources(counts, per_group):
    running = jnp.cumsum(counts, axis=1)
    slot_ids = jnp.arange(per_group, dtype=jnp.int32)
    return jnp.sum((running[:, None, :] <= slot_ids[None, :, None]).astype(jnp.int32), axis=2)


def local(
    in_panels,
    layout,
    hidden,
    prompt_state,
    fork_counts,
    conv_weight,
    conv_bias,
    x_weight,
    dt_weight,
    dt_bias,
    decay_rate,
    skip_gain,
):
    per_group, steps_count, local_width = hidden.shape
    whole = lax.all_gather(hidden, "tp", axis=2, tiled=True)
    model_width = whole.shape[2]
    row_count = per_group * steps_count
    panel_total = layout.shape[0]
    panel_rows = in_panels.shape[1]
    inner_local = in_panels.shape[3]
    blocks = whole.reshape(row_count, panel_total, panel_rows)
    ordered = jnp.take(blocks, layout, axis=1).reshape(row_count, model_width)
    piece = lax.all_gather(in_panels, "grp", axis=0, tiled=True)
    count = piece.shape[0]
    projected = jnp.dot(
        ordered,
        piece.reshape(count * panel_rows, 2 * inner_local),
        preferred_element_type=jnp.float32,
    )
    projected = projected.reshape(per_group, steps_count, 2, inner_local)
    x_in = projected[:, :, 0].astype(jnp.bfloat16)
    gate_z = projected[:, :, 1].astype(jnp.bfloat16)
    group_index = lax.axis_index("grp")
    own_counts = lax.dynamic_slice_in_dim(fork_counts, group_index, 1, 0)
    sources = fork_sources(own_counts, per_group)[0]
    piece = lax.all_gather(prompt_state, "grp", axis=0, tiled=True)
    prompt_ids = jnp.arange(piece.shape[0], dtype=jnp.int32)
    selector = (sources[:, None] == prompt_ids[None, :]).astype(jnp.float32)
    start_state = jnp.einsum("sp,pkc->skc", selector, piece, precision=lax.Precision.HIGHEST)
    taps = conv_weight.shape[0]
    window = jnp.concatenate([start_state[:, : taps - 1], x_in.astype(jnp.float32)], axis=1)
    conv_out = conv_bias + sum(
        (conv_weight[tap] * window[:, tap : tap + steps_count] for tap in range(taps))
    )
    xc = jax.nn.silu(conv_out).astype(jnp.bfloat16)
    partial_dbc = jnp.dot(
        xc.reshape(row_count, inner_local), x_weight, preferred_element_type=jnp.float32
    )
    dbc = lax.psum(partial_dbc, "tp")
    rank = dt_weight.shape[0]
    state_size = decay_rate.shape[0]
    dt_low = dbc[:, :rank].astype(jnp.bfloat16)
    b_in = dbc[:, rank : rank + state_size].reshape(per_group, steps_count, state_size)
    c_out = dbc[:, rank + state_size :].reshape(per_group, steps_count, state_size)
    step_size = jax.nn.softplus(
        jnp.dot(dt_low, dt_weight, preferred_element_type=jnp.float32) + dt_bias
    )
    step_size = step_size.reshape(per_group, steps_count, inner_local)

    def advance(state, inputs):
        step_now, b_now, c_now, xc_now, z_now = inputs
        xc_float = xc_now.astype(jnp.float32)
        decay = jnp.exp(-step_now[:, None, :] * decay_rate[None])
        state = decay * state + step_now[:, None, :] * b_now[:, :, None] * xc_float[:, None, :]
        output = jnp.sum(c_now[:, :, None] * state, axis=1) + skip_gain * xc_float
        output = output * jax.nn.silu(z_now.astype(jnp.float32))
        return (state, output.astype(jnp.bfloat16))

    inputs = (
        jnp.moveaxis(step_size, 1, 0),
        jnp.moveaxis(b_in, 1, 0),
        jnp.moveaxis(c_out, 1, 0),
        jnp.moveaxis(xc, 1, 0),
        jnp.moveaxis(gate_z, 1, 0),
    )
    state, outputs = lax.scan(advance, start_state[:, taps - 1 :], inputs)
    mixed = jnp.moveaxis(outputs, 0, 1)
    final_state = jnp.concatenate(
        [x_in[:, steps_count - (taps - 1) :].astype(jnp.float32), state], axis=1
    )
    return (mixed, final_state)


def solution(mesh):
    return jax.shard_map(
        local,
        mesh=mesh,
        in_specs=(
            P("grp", None, None, "tp"),
            P(),
            P("grp", None, "tp"),
            P("grp", None, "tp"),
            P(),
            P(None, "tp"),
            P("tp"),
            P("tp", None),
            P(None, "tp"),
            P("tp"),
            P(None, "tp"),
            P("tp"),
        ),
        out_specs=(P("grp", None, "tp"), P("grp", None, "tp")),
        check_vma=False,
    )
```

profile of v0, /device:TPU:26, one launch (start us, length us, event | category | flops | bytes accessed | tf_op | source)
XLA Modules:
  0.0 658.4 jit_solution(17948332740327699876)
XLA Ops:
  7.2 2.0 copy.109
  10.0 9.4 %copy.113 = bf16[2,1024,2,1024]{3,1,2,0:T(8,128)(2,1)} copy(bf16[2,1024,2,1024]{3,2,1,0:T(2,128)(2,1)} %param.14) | data formatting | bytes 16777216 | tf_op args[0]
  20.7 9.1 %all-gather.4.cloned.1.call-done = f32[16,19,1024]{2,1,0:T(8,128)} async-done(((f32[4,19,1024]{2,1,0:T(8,128)}), f32[16,19,1024]{2,1,0:T(8,128)}) %all-gather.4.cloned.1.call-update) | async-done | bytes 1245200 | tf_op jit(solution)/shard_map/all_gather | solution.py:49
  29.9 3.1 fusion.21
  35.2 120.8 %all-gather.6.cloned.1.call-done = bf16[32,16,8192]{2,1,0:T(8,128)(2,1)} async-done(((bf16[32,16,1024]{2,1,0:T(8,128)(2,1)}), bf16[32,16,8192]{2,1,0:T(8,128)(2,1)}) %all-gather.6.cloned.1.call-update) | async-done | bytes 8388624 | tf_op jit(solution)/shard_map/all_gather | solution.py:28
  156.0 17.9 %copy.126 = bf16[64,8,8,1024]{3,2,1,0:T(8,128)(2,1)} copy(bf16[64,8,8,1024]{3,1,2,0:T(8,128)(2,1)} %bitcast.77) | data formatting | bytes 16777216
  173.9 13.5 %copy.111 = bf16[512,8,1024]{2,0,1:T(8,128)(2,1)} copy(bf16[512,8,1024]{2,1,0:T(8,128)(2,1)} %bitcast.76) | data formatting | bytes 16777216 | tf_op jit(solution)/shard_map/reshape | solution.py:34
  187.4 8.2 %gather_fusion = bf16[8,512,1024]{2,1,0:T(8,128)(2,1)} fusion(bf16[512,8,1024]{2,0,1:T(8,128)(2,1)} %copy.111, s32[1024]{0:T(1024)S(1)} %pad_clamp_fusion), kind=kCustom, calls=%fused_computation | custom fusion | bytes 16777248 | tf_op jit(solution)/shard_map/jit(_take)/gather | solution.py:35
  195.6 7.5 %select_bitcast_fusion = bf16[512,8,1024]{2,0,1:T(8,128)(2,1)} fusion(bf16[8,512,1024]{2,1,0:T(8,128)(2,1)} %gather_fusion, pred[8]{0:T(512)(128)(4,1)S(1)} %compare_and_fusion), kind=kLoop, calls=%fused_computation.19 | loop fusion | flops 4194304 | bytes 16777224 | tf_op jit(solution)/shard_map/jit(_take)/select_n | solution.py:35
  203.1 11.3 %copy.112 = bf16[512,8,1024]{2,1,0:T(8,128)(2,1)} copy(bf16[512,8,1024]{2,0,1:T(8,128)(2,1)} %select_bitcast_fusion) | data formatting | bytes 16777216 | tf_op jit(solution)/shard_map/jit(_take)/select_n | solution.py:35
  214.4 13.6 %reshape.158 = bf16[32,16,8192,1]{2,1,0,3:T(8,128)(2,1)} reshape(bf16[512,8,1024]{2,1,0:T(8,128)(2,1)} %copy.112) | data formatting | bytes 16777216 | tf_op jit(solution)/shard_map/jit(_take)/select_n | solution.py:35
  228.0 130.4 %all-gather.8.cloned.1.call-done = bf16[8,1024,2,1024]{3,1,2,0:T(8,128)(2,1)} async-done(((bf16[2,1024,2,1024]{3,1,2,0:T(8,128)(2,1)}), bf16[8,1024,2,1024]{3,1,2,0:T(8,128)(2,1)}) %all-gather.8.cloned.1.call-update) | async-done | bytes 33554448 | tf_op jit(solution)/shard_map/all_gather | solution.py:36
  358.3 46.6 %copy.114 = bf16[8,1024,2,1024]{1,0,3,2:T(8,128)(2,1)} copy(bf16[8,1024,2,1024]{3,1,2,0:T(8,128)(2,1)} %all-gather.8.cloned.1.call-done) | data formatting | bytes 67108864 | tf_op jit(solution)/shard_map/all_gather | solution.py:36
  405.0 30.7 %copy.127 = bf16[256,8,8,1024]{3,1,2,0:T(8,128)(2,1)} copy(bf16[256,8,8,1024]{3,2,1,0:T(8,128)(2,1)} %bitcast.74) | data formatting | bytes 67108864
  435.6 29.1 %fusion.18 = bf16[32,16,2,1024]{3,0,1,2:T(8,128)(2,1)S(1)} fusion(bf16[2,1024,8192,1]{2,1,3,0:T(8,128)(2,1)} %bitcast.75, bf16[32,16,8192,1]{2,1,0,3:T(8,128)(2,1)} %reshape.158), kind=kOutput, calls=%fused_computation.38 | convolution fusion | flops 17180917760 | bytes 44040192 | tf_op jit(solution)/shard_map/dot_general | solution.py:38
  464.8 1.9 slice_bitcast_fusion.1
  469.6 1.8 fusion.30
  471.4 1.6 slice-done
  474.2 1.7 slice_convert_fusion.2
  475.9 74.3 %all-reduce.2.cloned.1.call-done = f32[512,544]{0,1:T(8,128)} async-done(((f32[512,544]{0,1:T(8,128)}), f32[512,544]{0,1:T(8,128)}) %all-reduce.2.cloned.1.call-update) | async-done | bytes 1114128 | tf_op jit(solution)/shard_map/psum | solution.py:62
  553.2 3.2 compare_select_fusion
  556.5 2.5 copy.136
  559.0 88.2 %while.12 = (s32[]{:T(128)}, f32[32,16,1024]{2,1,0:T(8,128)S(1)}, bf16[16,32,1024]{2,1,0:T(8,128)(2,1)}, f32[16,32,1024]{2,1,0:T(8,128)}, f32[16,1024]{1,0:T(8,1...) while((s32[]{:T(128)}, f32[32,16,1024]{2,1,0:T(8,128)S(1)}, ...), condition=%wide.region_5.6_spmd, body=%wide.region_3.5_spmd.sunk | while | flops 4030466 | bytes 5718649 | solution.py:89
  650.0 1.6 pad_maximum_fusion
  (132 shorter events, 102.2 us)
Async XLA Ops:
  7.2 462.4 %copy-start = (bf16[1024,544]{0,1:T(8,128)(2,1)S(1)}, bf16[1024,544]{0,1:T(8,128)(2,1)}, u32[]{:S(2)}) copy-start(bf16[1024,544]{0,1:T(8,128)(2,1)} %param.21) | copy-start | bytes 3342340
  7.2 22.7 %all-gather.4.cloned.1.call-start = ((), (), s32[]{:S(2)}) async-start(), calls=%async_computation | async-start | bytes 1966080 | tf_op jit(solution)/shard_map/all_gather | solution.py:49
  9.2 146.8 %all-gather.6.cloned.1.call-start = ((), (), s32[]{:S(2)}) async-start(), calls=%async_computation.1 | async-start | bytes 9437184 | tf_op jit(solution)/shard_map/all_gather | solution.py:28
  10.0 348.3 %all-gather.8.cloned.1.call-start = ((), (), s32[]{:S(2)}) async-start(), calls=%async_computation.2 | async-start | bytes 41943040 | tf_op jit(solution)/shard_map/all_gather | solution.py:36
  19.5 1.1 copy-start.11
  19.5 1.2 copy-start.8
  19.5 530.8 %all-reduce.2.cloned.1.call-start = ((), (), s32[]{:S(2)}) async-start(), calls=%async_computation.3 | async-start | bytes 2228224 | tf_op jit(solution)/shard_map/psum | solution.py:62
  33.0 1.5 copy-start.1
  464.8 1.9 copy-start.5
  464.8 1.9 copy-start.9
  468.0 1.0 copy-start.2
  471.4 1.6 slice-start
  474.2 79.1 %copy-start.10 = (f32[1024]{0:T(1024)S(1)}, f32[1024]{0:T(1024)}, u32[]{:S(2)}) copy-start(f32[1024]{0:T(1024)} %param.23) | copy-start | bytes 12292
  556.4 2.6 copy-start.3
  556.5 2.6 copy-start.7
  647.2 1.2 copy-start.6
  648.5 1.6 copy-start.4
Sparse Core Ops, SparseCore 0:
  10.1 19.6 all-gather.3
  32.1 123.8 all-gather.5
  157.6 200.7 all-gather.7
  471.5 78.7 all-reduce.1
where the time goes:
time: 669 us; the launch traced here: 658 us
  waiting for transfers between devices  335 us (50%)
  local copies, waits for them, and re-layouts  181 us (27%)
  other arithmetic  90.5 us (14%)
  matrix products  37.2 us (6%)
  between operations  14.1 us (2%)
    all_gather x1, waiting for transfers between devices, local(): piece = lax.all_gather(in_panels, 'grp', axis=0, tiled=True)  130 us
    all_gather x1, waiting for transfers between devices, local(): whole = lax.all_gather(hidden, 'tp', axis=2, tiled=True)  121 us
    psum x1, waiting for transfers between devices, local(): dbc = lax.psum(partial_dbc, 'tp')  74.3 us
    unnamed x28, local copies, waits for them, and re-layouts  62.5 us
    all_gather x1, local copies, waits for them, and re-layouts, local(): piece = lax.all_gather(in_panels, 'grp', axis=0, tiled=True)  46.6 us
    dot_general x1, matrix products, local(): jnp.dot(ordered, piece.reshape(count * panel_rows, 2 * inner_local), pref...  29.1 us
    dynamic_update_slice x16, other arithmetic, local(): state, outputs = lax.scan(advance, start_state[:, taps - 1:], inputs)  25 us
    select_n x2, local copies, waits for them, and re-layouts, local(): ordered = jnp.take(blocks, layout, axis=1).reshape(row_count, model_width)  24.9 us
  transfers between devices with their start and end apart: 4, of which 4 were waited for; matrix products, arithmetic and copies ran while one was open for 14% of the time, Pallas kernels for 0%

commit v1 on v0

v1 whole, which is shorter than its diff:
```python
import functools

import jax
import jax.numpy as jnp
from jax import lax
from jax.experimental import pallas as pl
from jax.experimental.pallas import tpu as pltpu
from jax.sharding import PartitionSpec as P

MESH = pl.DeviceIdType.MESH
MIB = 1024 * 1024


def fork_sources(counts, per_group):
    running = jnp.cumsum(counts, axis=1)
    slot_ids = jnp.arange(per_group, dtype=jnp.int32)
    return jnp.sum((running[:, None, :] <= slot_ids[None, :, None]).astype(jnp.int32), axis=2)


def ring_place(index, size):
    major, minor = index // 2, index % 2
    return jnp.where(minor == 0, major, size - 1 - major)


def ring_index(place, size):
    place = lax.rem(place + 2 * size, size)
    return jnp.where(place < size // 2, 2 * place, 2 * (size - 1 - place) + 1)


def meet(peers):
    barrier = pltpu.get_barrier_semaphore()
    for peer in peers:
        pl.semaphore_signal(barrier, inc=1, device_id=peer, device_id_type=MESH)
    pl.semaphore_wait(barrier, len(peers))


def project_kernel(
    groups, size, layout_ref, hid_ref, w_hbm, out_ref,
    w_ref, blocks, picked, act, send1, recv1, own, fin, recv2,
    w_sem, a_send, a_recv, b_send, b_recv, r_send, r_recv, s1_send, s1_recv, s2_send, s2_recv,
):
    grp, tp = lax.axis_index("grp"), lax.axis_index("tp")
    outers = groups // 2
    outer, core = grp // 2, grp % 2
    partner = outer * 2 + 1 - core
    parts, _, seqs, panel_rows = hid_ref.shape
    depth = 2 * panel_rows
    width = w_ref.shape[1]
    place = ring_place(tp, size)
    right, left = ring_index(place + 1, size), ring_index(place - 1, size)

    def remote(src, dst, send, recv, g, t):
        return pltpu.make_async_remote_copy(
            src_ref=src, dst_ref=dst, send_sem=send, recv_sem=recv,
            device_id=(g, t), device_id_type=MESH,
        )

    load_w = pltpu.make_async_copy(w_hbm, w_ref, w_sem)
    load_w.start()
    meet(
        [(grp, lax.rem(tp + d, size)) for d in range(1, size)]
        + [(lax.rem(grp + d, groups), tp) for d in range(1, groups)]
    )

    spread = []
    for d in range(1, size):
        to = lax.rem(tp + d, size)
        copy = remote(
            hid_ref.at[:, pl.ds(2 * to, 2)], blocks.at[pl.ds(tp * parts, parts)],
            a_send.at[d], a_recv.at[d], grp, to,
        )
        copy.start()
        spread.append(copy)
    blocks[pl.ds(tp * parts, parts)] = hid_ref[:, pl.ds(2 * tp, 2)]
    for copy in spread:
        copy.wait_recv()

    handed = []
    for d in range(1, groups + 1):
        to = lax.rem(grp + d, groups)
        for j in range(2):
            block = blocks[layout_ref[2 * to + j]]
            columns = slice(j * panel_rows, (j + 1) * panel_rows)
            if d < groups:
                picked[d - 1, :, :, columns] = block
            else:
                act[0, :, grp, :, columns] = block
        if d < groups:
            copy = remote(
                picked.at[d - 1], act.at[0, :, grp], b_send.at[d], b_recv.at[d], to, tp
            )
            copy.start()
            handed.append(copy)
    load_w.wait()
    for copy in handed:
        copy.wait_recv()

    def ring(step, way):
        return remote(
            act.at[step, way], act.at[step + 1, way],
            r_send.at[step, way], r_recv.at[step, way], grp, (right, left)[way],
        )

    def swap(step):
        return remote(
            send1, recv1.at[step], s1_send.at[step], s1_recv.at[step], partner, tp
        )

    def cross(step, d):
        to = lax.rem(outer + d, outers)
        return remote(
            recv1.at[step, :, to], recv2.at[step, d - 1],
            s2_send.at[step, d - 1], s2_recv.at[step, d - 1], to * 2 + core, tp,
        )

    tile = 512

    def turn(step, carry):
        @pl.when((step >= 1) & (step < size))
        def _():
            for way in range(2):
                ring(step - 1, way).wait_recv()

        @pl.when(step < size - 1)
        def _():
            for way in range(2):
                ring(step, way).start()

        @pl.when((step >= 1) & (step <= size))
        def _():
            at = step - 1
            swap(at).wait()
            for d in range(1, outers):
                to = lax.rem(outer + d, outers)
                total = own[:, to] + recv1[at, :, to].astype(jnp.float32)
                recv1[at, :, to] = total.astype(jnp.bfloat16)
                cross(at, d).start()
            fin[at % 2] = own[:, outer] + recv1[at, :, outer].astype(jnp.float32)

        @pl.when(step >= 2)
        def _():
            at = step - 2
            for d in range(1, outers):
                cross(at, d).wait_recv()
            total = fin[at % 2]
            for d in range(1, outers):
                total = total + recv2[at, d - 1].astype(jnp.float32)
            total = total.astype(jnp.bfloat16)
            out_ref[2 * ring_index(place - at, size)] = total[0]
            out_ref[2 * ring_index(place + at, size) + 1] = total[1]

        @pl.when(step < size)
        def _():
            @pl.loop(0, width // tile)
            def _(n):
                columns = pl.ds(pl.multiple_of(n * tile, tile), tile)
                rows = act[step].reshape(2 * groups * seqs, depth)
                value = jnp.dot(rows, w_ref[:, columns], preferred_element_type=jnp.float32)
                value = value.reshape(2, outers, 2, seqs, tile)
                first, second = value[:, :, 0], value[:, :, 1]
                own[:, :, :, columns] = jnp.where(core == 0, first, second)
                send1[:, :, :, columns] = jnp.where(core == 0, second, first).astype(jnp.bfloat16)

            swap(step).start()

        return carry

    lax.fori_loop(0, size + 2, turn, 0)

    for copy in spread + handed:
        copy.wait_send()

    def drain(step, carry):
        @pl.when(step < size - 1)
        def _():
            for way in range(2):
                ring(step, way).wait_send()

        for d in range(1, outers):
            cross(step, d).wait_send()
        return carry

    lax.fori_loop(0, size, drain, 0)


def project(layout, hid, weights, groups, size):
    parts, steps, per_step, panel_rows = hid.shape
    depth, width = weights.shape
    seqs = steps * per_step // (2 * size)
    hid = hid.reshape(parts, 2 * size, seqs, panel_rows)
    outers = groups // 2
    bf16, f32 = jnp.bfloat16, jnp.float32
    dma = pltpu.SemaphoreType.DMA
    vmem = pl.BlockSpec(memory_space=pltpu.VMEM)
    out = pl.pallas_call(
        functools.partial(project_kernel, groups, size),
        out_shape=jax.ShapeDtypeStruct((2 * size, seqs, width), bf16),
        in_specs=[
            pl.BlockSpec(memory_space=pltpu.SMEM), vmem, pl.BlockSpec(memory_space=pl.ANY),
        ],
        out_specs=vmem,
        scratch_shapes=[
            pltpu.VMEM((depth, width), bf16),
            pltpu.VMEM((parts * size, 2, seqs, panel_rows), bf16),
            pltpu.VMEM((groups - 1, 2, seqs, depth), bf16),
            pltpu.VMEM((size, 2, groups, seqs, depth), bf16),
            pltpu.VMEM((2, outers, seqs, width), bf16),
            pltpu.VMEM((size, 2, outers, seqs, width), bf16),
            pltpu.VMEM((2, outers, seqs, width), f32),
            pltpu.VMEM((2, 2, seqs, width), f32),
            pltpu.VMEM((size, outers - 1, 2, seqs, width), bf16),
            dma(()),
            dma((size,)), dma((size,)),
            dma((groups,)), dma((groups,)),
            dma((size, 2)), dma((size, 2)),
            dma((size,)), dma((size,)),
            dma((size, outers - 1)), dma((size, outers - 1)),
        ],
        compiler_params=pltpu.CompilerParams(
            collective_id=0, has_side_effects=True, vmem_limit_bytes=58 * MIB
        ),
        cost_estimate=pl.CostEstimate(
            flops=4 * groups * size * seqs * depth * width,
            bytes_accessed=16 * MIB, transcendentals=0,
        ),
    )(layout, hid, weights)
    return out.reshape(steps, per_step, width)


def mix_kernel(
    size, x_ref, start_ref, cw_ref, cb_ref, xw_ref, xc_ref, low_ref, bc_ref,
    win, p_low, p_bc, g_low, g_bc, l_send, l_recv, c_send, c_recv, ol_send, ol_recv, oc_send, oc_recv,
):
    grp, tp = lax.axis_index("grp"), lax.axis_index("tp")
    steps, seqs, channels = xc_ref.shape
    taps = cw_ref.shape[0]
    rank = low_ref.shape[2]
    each = steps // size

    meet([(grp, lax.rem(tp + d, size)) for d in range(1, size)])

    win[: taps - 1] = start_ref[...]
    win[taps - 1 :] = x_ref[...].astype(jnp.float32)

    def conv(t, carry):
        total = jnp.broadcast_to(cb_ref[...], (seqs, channels))
        for tap in range(taps):
            total = total + cw_ref[tap : tap + 1, :] * win[t + tap]
        xc_ref[t] = (total * jax.nn.sigmoid(total)).astype(jnp.bfloat16)
        return carry

    lax.fori_loop(0, steps, conv, 0)

    def remote(src, dst, send, recv, to):
        return pltpu.make_async_remote_copy(
            src_ref=src, dst_ref=dst, send_sem=send, recv_sem=recv,
            device_id=(grp, to), device_id_type=MESH,
        )

    rows = xc_ref[...].reshape(steps * seqs, channels)
    part = jnp.dot(rows, xw_ref[...], preferred_element_type=jnp.float32)
    part = part.reshape(steps, seqs, xw_ref.shape[1])
    p_low[...] = part[:, :, :rank].astype(jnp.bfloat16)
    p_bc[...] = part[:, :, rank:]

    gathers = []
    for d in range(1, size):
        to = lax.rem(tp + d, size)
        span = pl.ds(each * to, each)
        for copy in (
            remote(p_low.at[span], g_low.at[d], l_send.at[d], l_recv.at[d], to),
            remote(p_bc.at[span], g_bc.at[d], c_send.at[d], c_recv.at[d], to),
        ):
            copy.start()
            gathers.append(copy)
    mine = pl.ds(each * tp, each)
    for copy in gathers:
        copy.wait_recv()
    low = p_low[mine].astype(jnp.float32)
    bc = p_bc[mine]
    for d in range(1, size):
        low = low + g_low[d].astype(jnp.float32)
        bc = bc + g_bc[d]
    low_ref[mine] = low.astype(jnp.bfloat16)
    bc_ref[mine] = bc
    shares = []
    for d in range(1, size):
        to = lax.rem(tp + d, size)
        for copy in (
            remote(low_ref.at[mine], low_ref.at[mine], ol_send.at[d], ol_recv.at[d], to),
            remote(bc_ref.at[mine], bc_ref.at[mine], oc_send.at[d], oc_recv.at[d], to),
        ):
            copy.start()
            shares.append(copy)
    for copy in shares:
        copy.wait_recv()
    for copy in gathers + shares:
        copy.wait_send()


def mix(xz, start, conv_weight, conv_bias, x_weight, rank, size):
    steps, seqs, both = xz.shape
    channels = both // 2
    extra = 128
    each = steps // size
    bf16, f32 = jnp.bfloat16, jnp.float32
    dma = pltpu.SemaphoreType.DMA
    vmem = pl.BlockSpec(memory_space=pltpu.VMEM)
    x_weight = jnp.pad(x_weight, ((0, 0), (0, rank + extra - x_weight.shape[1])))
    return pl.pallas_call(
        functools.partial(mix_kernel, size),
        grid=(1,),
        out_shape=(
            jax.ShapeDtypeStruct((steps, seqs, channels), bf16),
            jax.ShapeDtypeStruct((steps, seqs, rank), bf16),
            jax.ShapeDtypeStruct((steps, seqs, extra), f32),
        ),
        in_specs=[
            pl.BlockSpec((steps, seqs, channels), lambda i: (0, 0, 0)),
            vmem, vmem, vmem, vmem,
        ],
        out_specs=[vmem] * 3,
        scratch_shapes=[
            pltpu.VMEM((start.shape[0] + steps, seqs, channels), f32),
            pltpu.VMEM((steps, seqs, rank), bf16),
            pltpu.VMEM((steps, seqs, extra), f32),
            pltpu.VMEM((size, each, seqs, rank), bf16),
            pltpu.VMEM((size, each, seqs, extra), f32),
        ]
        + [dma((size,))] * 8,
        compiler_params=pltpu.CompilerParams(
            collective_id=1, has_side_effects=True, vmem_limit_bytes=40 * MIB
        ),
    )(xz, start, conv_weight, conv_bias.reshape(1, channels), x_weight)


def scan_kernel(
    last_ref, z_ref, xc_ref, low_ref, bc_ref, start_ref, dtw_ref, dtb_ref, rate_ref, skip_ref,
    mixed_ref, final_ref, step_ref,
):
    steps, seqs, channels = xc_ref.shape
    states = rate_ref.shape[0]
    tail = last_ref.shape[0]
    rows = low_ref[...].reshape(steps * seqs, low_ref.shape[2])
    drive = jnp.dot(rows, dtw_ref[...], preferred_element_type=jnp.float32) + dtb_ref[...]
    drive = jnp.maximum(drive, 0.0) + jnp.log1p(jnp.exp(-jnp.abs(drive)))
    step_ref[...] = drive.reshape(steps, seqs, channels)
    final_ref[:tail] = last_ref[...].astype(jnp.float32)
    final_ref[tail:] = start_ref[...]

    def advance(t, carry):
        step = step_ref[t]
        xc = xc_ref[t].astype(jnp.float32)
        bc = bc_ref[t]
        push = step * xc
        output = skip_ref[...] * xc
        for n in range(states):
            decay = jnp.exp(-step * rate_ref[n : n + 1, :])
            state = decay * final_ref[tail + n] + push * bc[:, n : n + 1]
            final_ref[tail + n] = state
            output = output + bc[:, states + n : states + n + 1] * state
        z = z_ref[t].astype(jnp.float32)
        mixed_ref[t] = (output * (z * jax.nn.sigmoid(z))).astype(jnp.bfloat16)
        return carry

    lax.fori_loop(0, steps, advance, 0)


def scan(xz, xc, low, bc, start, dt_weight, dt_bias, decay_rate, skip_gain, tail):
    steps, seqs, channels = xc.shape
    states = decay_rate.shape[0]
    rank = low.shape[2]
    block = 256
    count = channels // block
    return pl.pallas_call(
        scan_kernel,
        grid=(count,),
        out_shape=(
            jax.ShapeDtypeStruct((steps, seqs, channels), jnp.bfloat16),
            jax.ShapeDtypeStruct((tail + states, seqs, channels), jnp.float32),
        ),
        in_specs=[
            pl.BlockSpec((tail, seqs, block), lambda i: (0, 0, i)),
            pl.BlockSpec((steps, seqs, block), lambda i: (0, 0, count + i)),
            pl.BlockSpec((steps, seqs, block), lambda i: (0, 0, i)),
            pl.BlockSpec((steps, seqs, rank), lambda i: (0, 0, 0)),
            pl.BlockSpec((steps, seqs, bc.shape[2]), lambda i: (0, 0, 0)),
            pl.BlockSpec((states, seqs, block), lambda i: (0, 0, i)),
            pl.BlockSpec((rank, block), lambda i: (0, i)),
            pl.BlockSpec((1, block), lambda i: (0, i)),
            pl.BlockSpec((states, block), lambda i: (0, i)),
            pl.BlockSpec((1, block), lambda i: (0, i)),
        ],
        out_specs=[
            pl.BlockSpec((steps, seqs, block), lambda i: (0, 0, i)),
            pl.BlockSpec((tail + states, seqs, block), lambda i: (0, 0, i)),
        ],
        scratch_shapes=[pltpu.VMEM((steps, seqs, block), jnp.float32)],
        compiler_params=pltpu.CompilerParams(vmem_limit_bytes=40 * MIB),
    )(
        xz[steps - tail :, :, :channels], xz, xc, low, bc, start, dt_weight,
        dt_bias.reshape(1, channels), decay_rate, skip_gain.reshape(1, channels),
    )


def local(
    groups,
    size,
    in_panels,
    layout,
    hidden,
    prompt_state,
    fork_counts,
    conv_weight,
    conv_bias,
    x_weight,
    dt_weight,
    dt_bias,
    decay_rate,
    skip_gain,
):
    seqs, steps, features = hidden.shape
    panels, panel_rows, _, channels = in_panels.shape
    taps = conv_weight.shape[0]
    rank = dt_weight.shape[0]
    prompts = lax.all_gather(prompt_state, "grp", axis=0, tiled=True)
    weights = in_panels.reshape(panels * panel_rows, 2 * channels)
    hid = hidden.reshape(seqs, steps, features // panel_rows, panel_rows).transpose(2, 1, 0, 3)
    own_counts = lax.dynamic_slice_in_dim(fork_counts, lax.axis_index("grp"), 1, 0)
    sources = fork_sources(own_counts, seqs)[0]
    prompt_ids = jnp.arange(prompts.shape[0], dtype=jnp.int32)
    selector = (sources[:, None] == prompt_ids[None, :]).astype(jnp.float32)
    start = jnp.einsum("sp,pkc->ksc", selector, prompts, precision=lax.Precision.HIGHEST)
    xz = project(layout, hid, weights, groups, size)
    xc, low, bc = mix(xz, start[: taps - 1], conv_weight, conv_bias, x_weight, rank, size)
    mixed, final = scan(
        xz, xc, low, bc, start[taps - 1 :], dt_weight, dt_bias, decay_rate, skip_gain, taps - 1
    )
    return mixed.transpose(1, 0, 2), final.transpose(1, 0, 2)


def solution(mesh):
    return jax.shard_map(
        functools.partial(local, mesh.shape["grp"], mesh.shape["tp"]),
        mesh=mesh,
        in_specs=(
            P("grp", None, None, "tp"),
            P(),
            P("grp", None, "tp"),
            P("grp", None, "tp"),
            P(),
            P(None, "tp"),
            P("tp"),
            P("tp", None),
            P(None, "tp"),
            P("tp"),
            P(None, "tp"),
            P("tp"),
        ),
        out_specs=(P("grp", None, "tp"), P("grp", None, "tp")),
        check_vma=False,
    )
```

time: 669 us -> 238 us (0.36); the launches traced: 658 us -> 238 us
  waiting for transfers between devices: 335 us -> 0.03 us
  Pallas kernels: 0 us -> 201 us
  local copies, waits for them, and re-layouts: 181 us -> 18.6 us
  other arithmetic: 90.5 us -> 0.28 us
  matrix products: 37.2 us -> 3.14 us
    all_gather x3 -> x1, waiting for transfers between devices: 260 us -> 0.02 us  [local(): prompts = lax.all_gather(prompt_state, 'grp', axis=0, tiled=True)]
    pallas_call x0 -> x3, Pallas kernels: none -> 201 us  [the longest x1 139 us: project(): pl.pallas_call(functools.partial(project_kernel, groups, size), out_shape...]
    psum x1 -> x0, waiting for transfers between devices: 74.3 us -> none  [local(): dbc = lax.psum(partial_dbc, 'tp')]
    all_gather x1 -> x0, local copies, waits for them, and re-layouts: 46.6 us -> none  [local(): piece = lax.all_gather(in_panels, 'grp', axis=0, tiled=True)]
    unnamed x28 -> x25, local copies, waits for them, and re-layouts: 62.5 us -> 17.3 us
    dot_general x4 -> x1, matrix products: 37.2 us -> 3.14 us  [local(): jnp.einsum('sp,pkc->ksc', selector, prompts, precision=lax.Precision.HIGH...]
    dynamic_update_slice x16 -> x0, other arithmetic: 25 us -> none  [local(): state, outputs = lax.scan(advance, start_state[:, taps - 1:], inputs)]
    select_n x2 -> x0, local copies, waits for them, and re-layouts: 24.9 us -> none  [local(): ordered = jnp.take(blocks, layout, axis=1).reshape(row_count, model_width)]
  transfers between devices with their start and end apart: 4 -> 1, of which waited for: 4 -> 0; matrix products, arithmetic and copies ran while one was open for 14% -> 6% of each run, Pallas kernels for 0% -> 58%
where the time goes in v1:
time: 238 us
  Pallas kernels  201 us (84%)
  local copies, waits for them, and re-layouts  18.6 us (8%)
  between operations  14.2 us (6%)
  matrix products  3.14 us (1%)
    pallas_call x1, Pallas kernels, project(): pl.pallas_call(functools.partial(project_kernel, groups, size), out_shape...  139 us
    pallas_call x1, Pallas kernels, mix(): pl.pallas_call(functools.partial(mix_kernel, size), grid=(1,), out_shape=...  42.1 us
    pallas_call x1, Pallas kernels, scan(): pl.pallas_call(scan_kernel, grid=(count,), out_shape=(jax.ShapeDtypeStruc...  20.3 us
    unnamed x25, local copies, waits for them, and re-layouts  17.3 us
  transfers between devices with their start and end apart: 1, of which 0 were waited for; matrix products, arithmetic and copies ran while one was open for 6% of the time, Pallas kernels for 58%

profile of v1, /device:TPU:26, one launch (start us, length us, event | category | flops | bytes accessed | tf_op | source)
XLA Modules:
  0.0 237.7 jit_solution(5746948925503925311)
XLA Ops:
  7.2 0.0 copy-start
  7.2 0.0 all-gather.2.cloned.1.call-start
  7.2 2.0 copy.23
  9.2 0.0 all-gather.2.cloned.1.call-update
  9.2 1.5 copy.31
  10.8 10.1 %copy.27 = bf16[256,8,2,1024]{3,1,2,0:T(8,128)(2,1)} copy(bf16[256,8,2,1024]{3,2,1,0:T(2,128)(2,1)} %bitcast.23) | data formatting | bytes 16777216
  20.9 138.9 %shard_map.131.x_ref.z_ref = bf16[16,32,2048]{2,1,0:T(8,128)(2,1)} custom-call(s32[8]{0:T(128)} %layout_ref.1, bf16[1,16,32,1024]{3,2,1,0:T(8,128)(2,1)} %bitcast.25, bf16[2048,2048]{1,0:T(8,128)(2,1)} %bitcast.24), custom_call_target="tpu_custom_call" | custom-call | flops 17179869184 | bytes 16777216 | tf_op jit(solution)/shard_map/pallas_call | solution.py:195
  159.9 0.9 slice.9.last_ref
  160.9 0.2 reduce_window_sum.11
  161.1 0.7 copy.25
  161.8 0.1 pad.4.xw_ref
  161.9 0.1 convert_reduce_fusion
  162.0 0.0 all-gather.2.cloned.1.call-done
  162.0 3.1 %convolution_bitcast_fusion = f32[19,32,1024]{2,1,0:T(8,128)S(1)} fusion(f32[16,19,1024]{2,1,0:T(8,128)} %all-gather.2.cloned.1.call-done, s32[32]{0:T(128)S(1)} %convert_reduce_fusion), kind=kOutput, calls=%fused_computation | convolution fusion | flops 119538176 | bytes 3735680 | tf_op jit(solution)/shard_map/sp,pkc->ksc/dot_general | solution.py:433
  165.2 0.0 copy-start.4
  165.2 0.0 copy-start.5
  165.2 0.2 slice.13.start_ref
  165.5 1.3 copy-done.1
  166.8 0.0 copy-done.5
  166.8 0.0 copy-start.6
  166.8 0.0 copy-start.7
  166.8 42.1 %shard_map.132 = (bf16[16,32,1024]{2,1,0:T(8,128)(2,1)S(1)}, bf16[16,32,512]{2,1,0:T(8,128)(2,1)S(1)}, f32[16,32,128]{2,1,0:T(8,128)S(1)}) custom-call(bf16[16,32,2048]{2,1,0:T(8,128)(2,1)S(1)} %copy-done.1, f32[3,32,1024]{2,1,0:T(8,128)S(1)} %slice.12.start_ref, f32[4,1024]{1,0:T(4,128)S(1)} %copy-done.4, f32[1,1024]{1,0:T(1,128)S(1)} %bitcast.20, ...), custom_call_target="tpu_custom_call" | custom-call | tf_op jit(solution)/shard_map/pallas_call | solution.py:310
  209.0 20.3 %shard_map.133 = (bf16[16,32,1024]{2,1,0:T(8,128)(2,1)S(1)}, f32[19,32,1024]{2,1,0:T(8,128)}) custom-call(bf16[3,32,1024]{2,1,0:T(8,128)(2,1)S(1)} %slice.9.last_ref, bf16[16,32,2048]{2,1,0:T(8,128)(2,1)S(1)} %copy-done.1, bf16[16,32,1024]{2,1,0:T(8,128)(2,1)S(1)} %get-tuple-element.7.xc_ref, bf16[16,32,512]{2,1,0:T(8,128)(2,1)S(1)} %get-tuple-element.8.low_ref, ...), custom_call_target="tpu_custom_call" | custom-call | tf_op jit(solution)/shard_map/pallas_call | solution.py:375
  229.3 1.5 copy.26
  (15 shorter events, 0.1 us)
Async XLA Ops:
  7.2 153.7 %copy-start = (s32[4,16]{1,0:T(4,128)S(1)}, s32[4,16]{1,0:T(4,128)}, u32[]{:S(2)}) copy-start(s32[4,16]{1,0:T(4,128)} %param.16) | copy-start | bytes 772
  7.2 2.1 copy-start.9
  7.2 154.8 %all-gather.2.cloned.1.call-start = ((), (), s32[]{:S(2)}) async-start(), calls=%async_computation | async-start | bytes 1966080 | tf_op jit(solution)/shard_map/all_gather | solution.py:426
  20.9 140.1 %copy-start.8 = (bf16[1024,544]{0,1:T(8,128)(2,1)S(1)}, bf16[1024,544]{0,1:T(8,128)(2,1)}, u32[]{:S(2)}) copy-start(bf16[1024,544]{0,1:T(8,128)(2,1)} %param.19) | copy-start | bytes 3342340
  165.2 1.6 copy-start.1
  165.2 1.6 copy-start.4
  165.2 1.6 copy-start.5
  166.8 42.2 %copy-start.2 = (bf16[512,1024]{1,0:T(8,128)(2,1)S(1)}, bf16[512,1024]{1,0:T(8,128)(2,1)}, u32[]{:S(2)}) copy-start(bf16[512,1024]{1,0:T(8,128)(2,1)} %dtw_ref.1) | copy-start | bytes 3145732
  166.8 42.2 %copy-start.3 = (f32[16,1024]{1,0:T(8,128)S(1)}, f32[16,1024]{1,0:T(8,128)}, u32[]{:S(2)}) copy-start(f32[16,1024]{1,0:T(8,128)} %rate_ref.1) | copy-start | bytes 196612
  166.8 42.2 %copy-start.6 = (f32[1024]{0:T(1024)S(1)}, f32[1024]{0:T(1024)}, u32[]{:S(2)}) copy-start(f32[1024]{0:T(1024)} %param.21) | copy-start | bytes 12292
  166.8 42.2 %copy-start.7 = (f32[1024]{0:T(1024)S(1)}, f32[1024]{0:T(1024)}, u32[]{:S(2)}) copy-start(f32[1024]{0:T(1024)} %param.23) | copy-start | bytes 12292
Sparse Core Ops, SparseCore 0:
  10.2 19.6 all-gather.1

commit v2 on v1

--- a/solution.py
+++ b/solution.py
@@ -1,4 +1,5 @@
 import functools
+import math
 
 import jax
 import jax.numpy as jnp
@@ -242,37 +243,47 @@
     win[: taps - 1] = start_ref[...]
     win[taps - 1 :] = x_ref[...].astype(jnp.float32)
 
-    def conv(t, carry):
-        total = jnp.broadcast_to(cb_ref[...], (seqs, channels))
-        for tap in range(taps):
-            total = total + cw_ref[tap : tap + 1, :] * win[t + tap]
-        xc_ref[t] = (total * jax.nn.sigmoid(total)).astype(jnp.bfloat16)
-        return carry
-
-    lax.fori_loop(0, steps, conv, 0)
-
     def remote(src, dst, send, recv, to):
         return pltpu.make_async_remote_copy(
             src_ref=src, dst_ref=dst, send_sem=send, recv_sem=recv,
             device_id=(grp, to), device_id_type=MESH,
         )
 
-    rows = xc_ref[...].reshape(steps * seqs, channels)
-    part = jnp.dot(rows, xw_ref[...], preferred_element_type=jnp.float32)
-    part = part.reshape(steps, seqs, xw_ref.shape[1])
-    p_low[...] = part[:, :, :rank].astype(jnp.bfloat16)
-    p_bc[...] = part[:, :, rank:]
-
+    def conv(first):
+        total = jnp.broadcast_to(cb_ref[...], (each, seqs, channels))
+        for tap in range(taps):
+            total = total + cw_ref[tap : tap + 1, :] * win[pl.ds(first + tap, each)]
+        value = (total * jax.nn.sigmoid(total)).astype(jnp.bfloat16)
+        xc_ref[pl.ds(first, each)] = value
+        return value.reshape(each * seqs, channels)
+
+    lanes = lax.broadcasted_iota(jnp.int32, (each, 8, xw_ref.shape[1] - rank), 2)
+    quarter = (xw_ref.shape[1] - rank) * 8 // seqs
     gathers = []
-    for d in range(1, size):
-        to = lax.rem(tp + d, size)
-        span = pl.ds(each * to, each)
-        for copy in (
-            remote(p_low.at[span], g_low.at[d], l_send.at[d], l_recv.at[d], to),
-            remote(p_bc.at[span], g_bc.at[d], c_send.at[d], c_recv.at[d], to),
-        ):
-            copy.start()
-            gathers.append(copy)
+    half = size // 2
+    for part in range(2):
+        offsets = range(1 + part * half, 1 + (part + 1) * half)
+        rows = jnp.concatenate([conv(each * lax.rem(tp + d, size)) for d in offsets], axis=0)
+        product = jnp.dot(rows, xw_ref[...], preferred_element_type=jnp.float32)
+        product = product.reshape(half, each, seqs, xw_ref.shape[1])
+        for i, d in enumerate(offsets):
+            to = lax.rem(tp + d, size)
+            span = pl.ds(each * to, each)
+            p_low[span] = product[i, :, :, :rank].astype(jnp.bfloat16)
+            packed = product[i, :, :8, rank:]
+            for q in range(1, seqs // 8):
+                packed = jnp.where(
+                    lanes < q * quarter, packed, product[i, :, q * 8 : q * 8 + 8, rank:]
+                )
+            p_bc[span] = packed
+            if d == size:
+                continue
+            for copy in (
+                remote(p_low.at[span], g_low.at[d], l_send.at[d], l_recv.at[d], to),
+                remote(p_bc.at[span], g_bc.at[d], c_send.at[d], c_recv.at[d], to),
+            ):
+                copy.start()
+                gathers.append(copy)
     mine = pl.ds(each * tp, each)
     for copy in gathers:
         copy.wait_recv()
@@ -301,19 +312,22 @@
 def mix(xz, start, conv_weight, conv_bias, x_weight, rank, size):
     steps, seqs, both = xz.shape
     channels = both // 2
-    extra = 128
+    repeats = seqs // 8
+    extra = (x_weight.shape[1] - rank) * repeats
     each = steps // size
     bf16, f32 = jnp.bfloat16, jnp.float32
     dma = pltpu.SemaphoreType.DMA
     vmem = pl.BlockSpec(memory_space=pltpu.VMEM)
-    x_weight = jnp.pad(x_weight, ((0, 0), (0, rank + extra - x_weight.shape[1])))
+    x_weight = jnp.concatenate(
+        [x_weight[:, :rank], jnp.tile(x_weight[:, rank:], (1, repeats))], axis=1
+    )
     return pl.pallas_call(
         functools.partial(mix_kernel, size),
         grid=(1,),
         out_shape=(
             jax.ShapeDtypeStruct((steps, seqs, channels), bf16),
             jax.ShapeDtypeStruct((steps, seqs, rank), bf16),
-            jax.ShapeDtypeStruct((steps, seqs, extra), f32),
+            jax.ShapeDtypeStruct((steps, 8, extra), f32),
         ),
         in_specs=[
             pl.BlockSpec((steps, seqs, channels), lambda i: (0, 0, 0)),
@@ -323,9 +337,9 @@
         scratch_shapes=[
             pltpu.VMEM((start.shape[0] + steps, seqs, channels), f32),
             pltpu.VMEM((steps, seqs, rank), bf16),
-            pltpu.VMEM((steps, seqs, extra), f32),
+            pltpu.VMEM((steps, 8, extra), f32),
             pltpu.VMEM((size, each, seqs, rank), bf16),
-            pltpu.VMEM((size, each, seqs, extra), f32),
+            pltpu.VMEM((size, each, 8, extra), f32),
         ]
         + [dma((size,))] * 8,
         compiler_params=pltpu.CompilerParams(
@@ -348,19 +362,31 @@
     final_ref[:tail] = last_ref[...].astype(jnp.float32)
     final_ref[tail:] = start_ref[...]
 
+    rate = rate_ref[...] * -math.log2(math.e)
+    pairs = 2 * states
+
     def advance(t, carry):
-        step = step_ref[t]
-        xc = xc_ref[t].astype(jnp.float32)
+        step_all = step_ref[t]
+        xc_all = xc_ref[t].astype(jnp.float32)
+        z = z_ref[t].astype(jnp.float32)
+        gate = z * jax.nn.sigmoid(z)
         bc = bc_ref[t]
-        push = step * xc
-        output = skip_ref[...] * xc
-        for n in range(states):
-            decay = jnp.exp(-step * rate_ref[n : n + 1, :])
-            state = decay * final_ref[tail + n] + push * bc[:, n : n + 1]
-            final_ref[tail + n] = state
-            output = output + bc[:, states + n : states + n + 1] * state
-        z = z_ref[t].astype(jnp.float32)
-        mixed_ref[t] = (output * (z * jax.nn.sigmoid(z))).astype(jnp.bfloat16)
+        outputs = []
+        for q in range(seqs // 8):
+            own = slice(q * 8, q * 8 + 8)
+            step, xc = step_all[own], xc_all[own]
+            push = step * xc
+            output = skip_ref[...] * xc
+            for n in range(states):
+                b_at, c_at = q * pairs + n, q * pairs + states + n
+                state = (
+                    jnp.exp2(step * rate[n : n + 1, :]) * final_ref[tail + n, own]
+                    + push * bc[:, b_at : b_at + 1]
+                )
+                final_ref[tail + n, own] = state
+                output = output + bc[:, c_at : c_at + 1] * state
+            outputs.append(output)
+        mixed_ref[t] = (jnp.concatenate(outputs, axis=0) * gate).astype(jnp.bfloat16)
         return carry
 
     lax.fori_loop(0, steps, advance, 0)
@@ -370,7 +396,7 @@
     steps, seqs, channels = xc.shape
     states = decay_rate.shape[0]
     rank = low.shape[2]
-    block = 256
+    block = min(channels, 512)
     count = channels // block
     return pl.pallas_call(
         scan_kernel,
@@ -384,7 +410,7 @@
             pl.BlockSpec((steps, seqs, block), lambda i: (0, 0, count + i)),
             pl.BlockSpec((steps, seqs, block), lambda i: (0, 0, i)),
             pl.BlockSpec((steps, seqs, rank), lambda i: (0, 0, 0)),
-            pl.BlockSpec((steps, seqs, bc.shape[2]), lambda i: (0, 0, 0)),
+            pl.BlockSpec(bc.shape, lambda i: (0, 0, 0)),
             pl.BlockSpec((states, seqs, block), lambda i: (0, 0, i)),
             pl.BlockSpec((rank, block), lambda i: (0, i)),
             pl.BlockSpec((1, block), lambda i: (0, i)),

time: 238 us -> 222 us (0.933)
  Pallas kernels: 201 us -> 185 us
    pallas_call x1, Pallas kernels: 42.1 us -> 32.8 us  [mix(): pl.pallas_call(functools.partial(mix_kernel, size), grid=(1,), out_shape=...]
    pallas_call x1, Pallas kernels: 20.3 us -> 13.7 us  [scan(): pl.pallas_call(scan_kernel, grid=(count,), out_shape=(jax.ShapeDtypeStruc...]
    unnamed x25 -> x23, local copies, waits for them, and re-layouts: 17.3 us -> 17.1 us
  transfers between devices with their start and end apart: 1 -> 1, of which waited for: 0 -> 0; matrix products, arithmetic and copies ran while one was open for 6% -> 6% of each run, Pallas kernels for 58% -> 63%
where the time goes in v2:
time: 222 us
  Pallas kernels  185 us (83%)
  local copies, waits for them, and re-layouts  18.5 us (8%)
  between operations  14.3 us (6%)
  matrix products  3.14 us (1%)
    pallas_call x1, Pallas kernels, project(): pl.pallas_call(functools.partial(project_kernel, groups, size), out_shape...  139 us
    pallas_call x1, Pallas kernels, mix(): pl.pallas_call(functools.partial(mix_kernel, size), grid=(1,), out_shape=...  32.8 us
    unnamed x23, local copies, waits for them, and re-layouts  17.1 us
    pallas_call x1, Pallas kernels, scan(): pl.pallas_call(scan_kernel, grid=(count,), out_shape=(jax.ShapeDtypeStruc...  13.7 us
  transfers between devices with their start and end apart: 1, of which 0 were waited for; matrix products, arithmetic and copies ran while one was open for 6% of the time, Pallas kernels for 63%

profile of v2, /device:TPU:26, one launch (start us, length us, event | category | flops | bytes accessed | tf_op | source)
XLA Modules:
  0.0 221.7 jit_solution(12241838223131573221)
XLA Ops:
  7.2 0.0 copy-start
  7.2 0.0 all-gather.2.cloned.1.call-start
  7.2 2.0 copy.29
  9.2 0.0 all-gather.2.cloned.1.call-update
  9.2 1.5 copy.39
  10.8 10.1 %copy.35 = bf16[256,8,2,1024]{3,1,2,0:T(8,128)(2,1)} copy(bf16[256,8,2,1024]{3,2,1,0:T(2,128)(2,1)} %bitcast.24) | data formatting | bytes 16777216
  20.9 138.9 %shard_map.131.x_ref.z_ref = bf16[16,32,2048]{2,1,0:T(8,128)(2,1)} custom-call(s32[8]{0:T(128)} %layout_ref.1, bf16[1,16,32,1024]{3,2,1,0:T(8,128)(2,1)} %bitcast.27, bf16[2048,2048]{1,0:T(8,128)(2,1)} %bitcast.25), custom_call_target="tpu_custom_call" | custom-call | flops 17179869184 | bytes 16777216 | tf_op jit(solution)/shard_map/pallas_call | solution.py:196
  159.9 0.9 slice.15.last_ref
  160.9 0.2 reduce_window_sum.11
  161.1 0.2 copy.32
  161.3 0.5 copy.34
  161.8 0.1 convert_reduce_fusion
  161.9 0.1 pad_maximum_fusion.xw_ref
  162.0 0.0 all-gather.2.cloned.1.call-done
  162.0 3.1 %convolution_bitcast_fusion = f32[19,32,1024]{2,1,0:T(8,128)S(1)} fusion(f32[16,19,1024]{2,1,0:T(8,128)} %all-gather.2.cloned.1.call-done, s32[32]{0:T(128)S(1)} %convert_reduce_fusion), kind=kOutput, calls=%fused_computation | convolution fusion | flops 119538176 | bytes 3735680 | tf_op jit(solution)/shard_map/sp,pkc->ksc/dot_general | solution.py:459
  165.2 0.0 copy-start.4
  165.3 0.0 copy-start.5
  165.3 0.2 slice.21.start_ref
  165.5 0.0 copy-start.3
  165.5 0.0 copy-start.6
  165.6 1.3 copy-done.1
  166.8 32.8 %shard_map.132 = (bf16[16,32,1024]{2,1,0:T(8,128)(2,1)S(1)}, bf16[16,32,512]{2,1,0:T(8,128)(2,1)S(1)}, f32[16,8,128]{2,1,0:T(8,128)S(1)}) custom-call(bf16[16,32,2048]{2,1,0:T(8,128)(2,1)S(1)} %copy-done.1, f32[3,32,1024]{2,1,0:T(8,128)S(1)} %slice.20.start_ref, f32[4,1024]{1,0:T(4,128)S(1)} %copy-done.4, f32[1,1024]{1,0:T(1,128)S(1)} %bitcast.21, ...), custom_call_target="tpu_custom_call" | custom-call | tf_op jit(solution)/shard_map/pallas_call | solution.py:324
  199.7 13.7 %shard_map.133 = (bf16[16,32,1024]{2,1,0:T(8,128)(2,1)S(1)}, f32[19,32,1024]{2,1,0:T(8,128)}) custom-call(bf16[3,32,1024]{2,1,0:T(8,128)(2,1)S(1)} %slice.15.last_ref, bf16[16,32,2048]{2,1,0:T(8,128)(2,1)S(1)} %copy-done.1, bf16[16,32,1024]{2,1,0:T(8,128)(2,1)S(1)} %get-tuple-element.7.xc_ref, bf16[16,32,512]{2,1,0:T(8,128)(2,1)S(1)} %get-tuple-element.8.low_ref, ...), custom_call_target="tpu_custom_call" | custom-call | tf_op jit(solution)/shard_map/pallas_call | solution.py:401
  213.3 1.5 copy.33
  (19 shorter events, 0.1 us)
Async XLA Ops:
  7.2 153.7 %copy-start = (s32[4,16]{1,0:T(4,128)S(1)}, s32[4,16]{1,0:T(4,128)}, u32[]{:S(2)}) copy-start(s32[4,16]{1,0:T(4,128)} %param.16) | copy-start | bytes 772
  7.2 2.1 copy-start.8
  7.2 154.9 %all-gather.2.cloned.1.call-start = ((), (), s32[]{:S(2)}) async-start(), calls=%async_computation | async-start | bytes 1966080 | tf_op jit(solution)/shard_map/all_gather | solution.py:452
  20.9 140.1 %slice-start = ((bf16[1024,544]{0,1:T(8,128)(2,1)}), bf16[1024,32]{0,1:T(8,128)(2,1)S(1)}, s32[]{:S(2)}) async-start(bf16[1024,544]{0,1:T(8,128)(2,1)} %param.19), calls=%async_computation.1 | async-start | bytes 131072 | tf_op jit(solution)/shard_map/slice | solution.py:322
  20.9 140.3 %slice-start.1 = ((bf16[1024,544]{0,1:T(8,128)(2,1)}), bf16[1024,512]{0,1:T(8,128)(2,1)S(1)}, s32[]{:S(2)}) async-start(bf16[1024,544]{0,1:T(8,128)(2,1)} %param.19), calls=%async_computation.2 | async-start | bytes 2097152 | tf_op jit(solution)/shard_map/slice | solution.py:322
  165.2 1.6 copy-start.1
  165.2 1.6 copy-start.4
  165.3 1.6 copy-start.5
  165.5 34.1 %copy-start.2 = (bf16[512,1024]{1,0:T(8,128)(2,1)S(1)}, bf16[512,1024]{1,0:T(8,128)(2,1)}, u32[]{:S(2)}) copy-start(bf16[512,1024]{1,0:T(8,128)(2,1)} %dtw_ref.1) | copy-start | bytes 3145732
  165.5 34.1 %copy-start.3 = (f32[16,1024]{1,0:T(8,128)S(1)}, f32[16,1024]{1,0:T(8,128)}, u32[]{:S(2)}) copy-start(f32[16,1024]{1,0:T(8,128)} %rate_ref.1) | copy-start | bytes 196612
  165.5 34.1 %copy-start.6 = (f32[1024]{0:T(1024)S(1)}, f32[1024]{0:T(1024)}, u32[]{:S(2)}) copy-start(f32[1024]{0:T(1024)} %param.21) | copy-start | bytes 12292
  165.5 34.1 %copy-start.7 = (f32[1024]{0:T(1024)S(1)}, f32[1024]{0:T(1024)}, u32[]{:S(2)}) copy-start(f32[1024]{0:T(1024)} %param.23) | copy-start | bytes 12292
Sparse Core Ops, SparseCore 0:
  10.2 19.6 all-gather.1

commit v3 on v2

--- a/solution.py
+++ b/solution.py
@@ -37,7 +37,7 @@
 
 def project_kernel(
     groups, size, layout_ref, hid_ref, w_hbm, out_ref,
-    w_ref, blocks, picked, act, send1, recv1, own, fin, recv2,
+    w_ref, raw, blocks_a, blocks_b, picked, act, send1, recv1, own, fin, recv2,
     w_sem, a_send, a_recv, b_send, b_recv, r_send, r_recv, s1_send, s1_recv, s2_send, s2_recv,
 ):
     grp, tp = lax.axis_index("grp"), lax.axis_index("tp")
@@ -56,51 +56,78 @@
             device_id=(g, t), device_id_type=MESH,
         )
 
-    load_w = pltpu.make_async_copy(w_hbm, w_ref, w_sem)
+    load_w = pltpu.make_async_copy(w_hbm, raw, w_sem)
     load_w.start()
     meet(
         [(grp, lax.rem(tp + d, size)) for d in range(1, size)]
         + [(lax.rem(grp + d, groups), tp) for d in range(1, groups)]
     )
 
-    spread = []
-    for d in range(1, size):
-        to = lax.rem(tp + d, size)
-        copy = remote(
-            hid_ref.at[:, pl.ds(2 * to, 2)], blocks.at[pl.ds(tp * parts, parts)],
-            a_send.at[d], a_recv.at[d], grp, to,
-        )
-        copy.start()
-        spread.append(copy)
-    blocks[pl.ds(tp * parts, parts)] = hid_ref[:, pl.ds(2 * tp, 2)]
-    for copy in spread:
-        copy.wait_recv()
-
-    handed = []
-    for d in range(1, groups + 1):
-        to = lax.rem(grp + d, groups)
-        for j in range(2):
-            block = blocks[layout_ref[2 * to + j]]
-            columns = slice(j * panel_rows, (j + 1) * panel_rows)
-            if d < groups:
-                picked[d - 1, :, :, columns] = block
-            else:
-                act[0, :, grp, :, columns] = block
-        if d < groups:
+    blocks = (blocks_a, blocks_b)
+    spread = ([], [])
+    for way in range(2):
+        for d in range(1, size):
+            to = lax.rem(tp + d, size)
             copy = remote(
-                picked.at[d - 1], act.at[0, :, grp], b_send.at[d], b_recv.at[d], to, tp
+                hid_ref.at[:, 2 * to + way], blocks[way].at[pl.ds(tp * parts, parts)],
+                a_send.at[way, d], a_recv.at[way, d], grp, to,
             )
             copy.start()
-            handed.append(copy)
+            spread[way].append(copy)
+        blocks[way][pl.ds(tp * parts, parts)] = hid_ref[:, 2 * tp + way]
+
     load_w.wait()
-    for copy in handed:
-        copy.wait_recv()
+    run = 2 * width // 256 * 16
+    kinds = run // 16
+    order = lax.broadcasted_iota(jnp.int32, (run, run), 0)
+    source = lax.broadcasted_iota(jnp.int32, (run, run), 1)
+    wanted = (order % 16) * kinds + (order // 16)
+    sort = (source == wanted).astype(jnp.bfloat16)
+
+    @pl.loop(0, depth // 32)
+    def _(at):
+        pair = jnp.concatenate(
+            [raw[pl.ds(pl.multiple_of((2 * at + i) * run, run), run)] for i in range(2)], axis=1
+        )
+        tidy = jnp.dot(sort, pair, preferred_element_type=jnp.float32).astype(jnp.bfloat16)
+        for i in range(2):
+            rows = pl.ds(pl.multiple_of((2 * at + i) * 16, 16), 16)
+            for kind in range(kinds):
+                column = (kind % 2) * (width // 2) + (kind // 2) * 128
+                w_ref[rows, column : column + 128] = tidy[
+                    kind * 16 : kind * 16 + 16, i * 128 : i * 128 + 128
+                ]
 
     def ring(step, way):
         return remote(
             act.at[step, way], act.at[step + 1, way],
             r_send.at[step, way], r_recv.at[step, way], grp, (right, left)[way],
         )
+
+    handed = ([], [])
+    for way in range(2):
+        for copy in spread[way]:
+            copy.wait_recv()
+        for d in range(1, groups + 1):
+            to = lax.rem(grp + d, groups)
+            for j in range(2):
+                block = blocks[way][layout_ref[2 * to + j]]
+                columns = slice(j * panel_rows, (j + 1) * panel_rows)
+                if d < groups:
+                    picked[d - 1, way, :, columns] = block
+                else:
+                    act[0, way, grp, :, columns] = block
+            if d < groups:
+                copy = remote(
+                    picked.at[d - 1, way], act.at[0, way, grp],
+                    b_send.at[way, d], b_recv.at[way, d], to, tp,
+                )
+                copy.start()
+                handed[way].append(copy)
+    for way in range(2):
+        for copy in handed[way]:
+            copy.wait_recv()
+        ring(0, way).start()
 
     def swap(step):
         return remote(
@@ -122,10 +149,9 @@
             for way in range(2):
                 ring(step - 1, way).wait_recv()
 
-        @pl.when(step < size - 1)
-        def _():
-            for way in range(2):
-                ring(step, way).start()
+                @pl.when(step < size - 1)
+                def _():
+                    ring(step, way).start()
 
         @pl.when((step >= 1) & (step <= size))
         def _():
@@ -168,7 +194,7 @@
 
     lax.fori_loop(0, size + 2, turn, 0)
 
-    for copy in spread + handed:
+    for copy in spread[0] + spread[1] + handed[0] + handed[1]:
         copy.wait_send()
 
     def drain(step, carry):
@@ -186,7 +212,7 @@
 
 def project(layout, hid, weights, groups, size):
     parts, steps, per_step, panel_rows = hid.shape
-    depth, width = weights.shape
+    depth, width = 2 * panel_rows, weights.shape[0] * 128 // (2 * panel_rows)
     seqs = steps * per_step // (2 * size)
     hid = hid.reshape(parts, 2 * size, seqs, panel_rows)
     outers = groups // 2
@@ -202,7 +228,9 @@
         out_specs=vmem,
         scratch_shapes=[
             pltpu.VMEM((depth, width), bf16),
-            pltpu.VMEM((parts * size, 2, seqs, panel_rows), bf16),
+            pltpu.VMEM(weights.shape, bf16),
+            pltpu.VMEM((parts * size, seqs, panel_rows), bf16),
+            pltpu.VMEM((parts * size, seqs, panel_rows), bf16),
             pltpu.VMEM((groups - 1, 2, seqs, depth), bf16),
             pltpu.VMEM((size, 2, groups, seqs, depth), bf16),
             pltpu.VMEM((2, outers, seqs, width), bf16),
@@ -211,8 +239,8 @@
             pltpu.VMEM((2, 2, seqs, width), f32),
             pltpu.VMEM((size, outers - 1, 2, seqs, width), bf16),
             dma(()),
-            dma((size,)), dma((size,)),
-            dma((groups,)), dma((groups,)),
+            dma((2, size)), dma((2, size)),
+            dma((2, groups)), dma((2, groups)),
             dma((size, 2)), dma((size, 2)),
             dma((size,)), dma((size,)),
             dma((size, outers - 1)), dma((size, outers - 1)),
@@ -450,7 +478,8 @@
     taps = conv_weight.shape[0]
     rank = dt_weight.shape[0]
     prompts = lax.all_gather(prompt_state, "grp", axis=0, tiled=True)
-    weights = in_panels.reshape(panels * panel_rows, 2 * channels)
+    weights = in_panels.reshape(panels * panel_rows, 2, channels // 128, 128)
+    weights = weights.transpose(0, 2, 1, 3).reshape(-1, 128)
     hid = hidden.reshape(seqs, steps, features // panel_rows, panel_rows).transpose(2, 1, 0, 3)
     own_counts = lax.dynamic_slice_in_dim(fork_counts, lax.axis_index("grp"), 1, 0)
     sources = fork_sources(own_counts, seqs)[0]

time: 222 us -> 212 us (0.955)
  local copies, waits for them, and re-layouts: 18.5 us -> 9.1 us
    unnamed x23 -> x22, local copies, waits for them, and re-layouts: 17.1 us -> 7.79 us
    pallas_call x1, Pallas kernels: 139 us -> 136 us  [project(): pl.pallas_call(functools.partial(project_kernel, groups, size), out_shape...]
  transfers between devices with their start and end apart: 1 -> 1, of which waited for: 0 -> 0; matrix products, arithmetic and copies ran while one was open for 6% -> 2% of each run, Pallas kernels for 63% -> 65%
where the time goes in v3:
time: 212 us; the launch traced here: 211 us
  Pallas kernels  185 us (87%)
  between operations  14.2 us (7%)
  local copies, waits for them, and re-layouts  9.1 us (4%)
  matrix products  3.14 us (1%)
    pallas_call x1, Pallas kernels, project(): pl.pallas_call(functools.partial(project_kernel, groups, size), out_shape...  136 us
    pallas_call x1, Pallas kernels, mix(): pl.pallas_call(functools.partial(mix_kernel, size), grid=(1,), out_shape=...  34.4 us
    pallas_call x1, Pallas kernels, scan(): pl.pallas_call(scan_kernel, grid=(count,), out_shape=(jax.ShapeDtypeStruc...  13.7 us
    unnamed x22, local copies, waits for them, and re-layouts  7.79 us
  transfers between devices with their start and end apart: 1, of which 0 were waited for; matrix products, arithmetic and copies ran while one was open for 2% of the time, Pallas kernels for 65%

profile of v3, /device:TPU:26, one launch (start us, length us, event | category | flops | bytes accessed | tf_op | source)
XLA Modules:
  0.0 211.5 jit_solution(11664369513269682375)
XLA Ops:
  7.2 0.0 copy-start
  7.2 0.0 slice-start
  7.2 0.0 all-gather.2.cloned.1.call-start
  7.2 1.9 copy.33
  9.1 0.0 all-gather.2.cloned.1.call-update
  9.2 0.0 copy-start.8
  9.2 0.2 reduce_window_sum.11
  9.4 0.2 copy.36
  9.6 0.8 copy-done.8
  10.4 1.5 copy.42
  11.9 136.4 %shard_map.131.x_ref.z_ref = bf16[16,32,2048]{2,1,0:T(8,128)(2,1)} custom-call(s32[8]{0:T(128)} %layout_ref.1, bf16[1,16,32,1024]{3,2,1,0:T(8,128)(2,1)} %bitcast.27, bf16[32768,128]{1,0:T(8,128)(2,1)} %bitcast.28), custom_call_target="tpu_custom_call" | custom-call | flops 17179869184 | bytes 16777216 | tf_op jit(solution)/shard_map/pallas_call | solution.py:222
  148.4 0.9 slice.15.last_ref
  149.3 0.5 copy.38
  149.9 0.1 convert_reduce_fusion
  150.0 0.1 pad_maximum_fusion.xw_ref
  150.1 0.0 all-gather.2.cloned.1.call-done
  150.1 3.1 %convolution_bitcast_fusion = f32[19,32,1024]{2,1,0:T(8,128)S(1)} fusion(f32[16,19,1024]{2,1,0:T(8,128)} %all-gather.2.cloned.1.call-done, s32[32]{0:T(128)S(1)} %convert_reduce_fusion), kind=kOutput, calls=%fused_computation | convolution fusion | flops 119538176 | bytes 3735680 | tf_op jit(solution)/shard_map/sp,pkc->ksc/dot_general | solution.py:488
  153.3 0.0 copy-start.4
  153.3 0.1 slice.21.start_ref
  153.5 1.4 copy-done.1
  154.9 0.0 copy-start.7
  154.9 34.4 %shard_map.132 = (bf16[16,32,1024]{2,1,0:T(8,128)(2,1)S(1)}, bf16[16,32,512]{2,1,0:T(8,128)(2,1)S(1)}, f32[16,8,128]{2,1,0:T(8,128)S(1)}) custom-call(bf16[16,32,2048]{2,1,0:T(8,128)(2,1)S(1)} %copy-done.1, f32[3,32,1024]{2,1,0:T(8,128)S(1)} %slice.20.start_ref, f32[4,1024]{1,0:T(4,128)S(1)} %copy-done.4, f32[1,1024]{1,0:T(1,128)S(1)} %bitcast.23, ...), custom_call_target="tpu_custom_call" | custom-call | tf_op jit(solution)/shard_map/pallas_call | solution.py:352
  189.4 13.7 %shard_map.133 = (bf16[16,32,1024]{2,1,0:T(8,128)(2,1)S(1)}, f32[19,32,1024]{2,1,0:T(8,128)}) custom-call(bf16[3,32,1024]{2,1,0:T(8,128)(2,1)S(1)} %slice.15.last_ref, bf16[16,32,2048]{2,1,0:T(8,128)(2,1)S(1)} %copy-done.1, bf16[16,32,1024]{2,1,0:T(8,128)(2,1)S(1)} %get-tuple-element.7.xc_ref, bf16[16,32,512]{2,1,0:T(8,128)(2,1)S(1)} %get-tuple-element.8.low_ref, ...), custom_call_target="tpu_custom_call" | custom-call | tf_op jit(solution)/shard_map/pallas_call | solution.py:429
  203.1 1.5 copy.37
  (18 shorter events, 0.1 us)
Async XLA Ops:
  7.2 2.0 copy-start
  7.2 2.2 %slice-start = ((bf16[1024,544]{0,1:T(8,128)(2,1)}), bf16[1024,32]{0,1:T(8,128)(2,1)S(1)}, s32[]{:S(2)}) async-start(bf16[1024,544]{0,1:T(8,128)(2,1)} %param.19), calls=%async_computation.1 | async-start | bytes 131072 | tf_op jit(solution)/shard_map/slice | solution.py:350
  7.2 142.9 %all-gather.2.cloned.1.call-start = ((), (), s32[]{:S(2)}) async-start(), calls=%async_computation | async-start | bytes 1966080 | tf_op jit(solution)/shard_map/all_gather | solution.py:480
  9.2 1.2 copy-start.8
  11.9 137.4 %slice-start.1 = ((bf16[1024,544]{0,1:T(8,128)(2,1)}), bf16[1024,512]{0,1:T(8,128)(2,1)S(1)}, s32[]{:S(2)}) async-start(bf16[1024,544]{0,1:T(8,128)(2,1)} %param.19), calls=%async_computation.2 | async-start | bytes 2097152 | tf_op jit(solution)/shard_map/slice | solution.py:350
  153.3 1.6 copy-start.1
  153.3 1.6 copy-start.4
  153.3 1.6 copy-start.5
  154.9 34.5 %copy-start.2 = (bf16[512,1024]{1,0:T(8,128)(2,1)S(1)}, bf16[512,1024]{1,0:T(8,128)(2,1)}, u32[]{:S(2)}) copy-start(bf16[512,1024]{1,0:T(8,128)(2,1)} %dtw_ref.1) | copy-start | bytes 3145732
  154.9 34.5 %copy-start.3 = (f32[16,1024]{1,0:T(8,128)S(1)}, f32[16,1024]{1,0:T(8,128)}, u32[]{:S(2)}) copy-start(f32[16,1024]{1,0:T(8,128)} %rate_ref.1) | copy-start | bytes 196612
  154.9 34.5 %copy-start.6 = (f32[1024]{0:T(1024)S(1)}, f32[1024]{0:T(1024)}, u32[]{:S(2)}) copy-start(f32[1024]{0:T(1024)} %param.21) | copy-start | bytes 12292
  154.9 34.5 %copy-start.7 = (f32[1024]{0:T(1024)S(1)}, f32[1024]{0:T(1024)}, u32[]{:S(2)}) copy-start(f32[1024]{0:T(1024)} %param.23) | copy-start | bytes 12292
Sparse Core Ops, SparseCore 0:
  10.2 19.6 all-gather.1
